TPU v7x, 256 devices: a whole 4x4x8 slice. The times are simulated.
256 devices in a mesh: fsdp: 32 (over x, z), mp: 8 (over y, core).
Axes of the slice: x: 4, y: 4, z: 8, core: 2. Of those that a mesh axis runs over, the one named last changes fastest.
Arguments:
- grad: float32 [256, 512, 512], P('mp', 'fsdp')
- block_slot: int32 [256], P('mp'), may hold values from 0 to 63, as said below
- left_stat: float32 [64, 8, 512, 512], P('fsdp', 'mp')
- right_stat: float32 [64, 8, 512, 512], P('fsdp', 'mp')
- left_root: bfloat16 [64, 8, 512, 512], P('fsdp', 'mp')
- right_root: bfloat16 [64, 8, 512, 512], P('fsdp', 'mp')
Outputs:
- update: float32 [256, 512, 512], P('mp', 'fsdp')
- new_left: float32 [64, 8, 512, 512], P('fsdp', 'mp')
- new_right: float32 [64, 8, 512, 512], P('fsdp', 'mp')
Inputs may be any that keep to these rules, and one draw needn't show every extreme that they name: `block_slot`: within each tensor-parallel group no slot is named twice; slot s belongs to fsdp owner s // 2, so an owner gets at most 2 blocks, and in every group some owner gets exactly 2.
All inputs are finite; a program needn't handle non-finite values.
Results may differ from a plain program's by a relative error of at most 0.017.
Values sent between devices are 32-bit elements; how exact they have to be, the bound alone decides.
A program may use at most 64 MiB of HBM per device.

v0:
```python
import functools

import jax
import jax.numpy as jnp
from jax import lax
from jax.experimental import pallas as pl
from jax.experimental.pallas import tpu as pltpu
from jax.sharding import PartitionSpec as P

decay_rate = 0.9
epsilon = 1e-06
MESH = pl.DeviceIdType.MESH
F32 = jnp.float32
BF16 = jnp.bfloat16


def split(x):
    high = x.astype(BF16)
    return high, (x - high.astype(F32)).astype(BF16)


def dot(a, b, a_dim=1, b_dim=0):
    return lax.dot_general(a, b, (((a_dim,), (b_dim,)), ((), ())), preferred_element_type=F32)


def kernel(
    cfg,
    slot_hbm,
    grad_hbm,
    ls_hbm,
    rs_hbm,
    lr_hbm,
    rr_hbm,
    update,
    ls,
    rs,
    back,
    slot,
    table,
    source,
    grad,
    stage,
    blocks,
    dirs,
    lr,
    rr,
    high,
    low,
    sq_out,
    sq_group,
    sq_sum,
    sq_all,
    in_sem,
    fsend,
    frecv,
    rsend,
    rrecv,
    qsend,
    qrecv,
):
    fs, mps, cap, rows, width, inner, entries = cfg
    outer = fs // inner
    me = lax.axis_index("fsdp")
    lane = lax.axis_index("mp")
    me_out, me_in = me // inner, me % inner
    tile = 128
    tiles = width // tile

    turn = 1 - 2 * (me_in % 2)

    def zigzag(k, size):
        return (k + 1) // 2 if k % 2 else (size - k // 2) % size

    outs = [((me_out + turn * zigzag(k, outer) + outer) % outer) * inner for k in range(outer)]
    ins = [(me_in + turn * zigzag(k, inner) + inner) % inner for k in range(inner)]
    peers = [outs[d // inner] + ins[d % inner] for d in range(fs)]
    lanes = [(lane + d) % mps for d in range(mps)]

    def peer(d):
        k, j = d // inner, d % inner
        k = (k % 2) * ((k + 1) // 2) + (1 - k % 2) * (outer - k // 2)
        j = (j % 2) * ((j + 1) // 2) + (1 - j % 2) * (inner - j // 2)
        p_out = (me_out + turn * k + outer) % outer
        return p_out * inner + (me_in + turn * j + inner) % inner

    def rows_of(device):
        return pl.ds(pl.multiple_of(device * rows, rows), rows)

    pairs = (
        (slot_hbm, slot),
        (grad_hbm, grad),
        (lr_hbm, lr),
        (rr_hbm, rr),
        (ls_hbm, ls),
        (rs_hbm, rs),
    )
    loads = [pltpu.make_async_copy(a, b, in_sem.at[i]) for i, (a, b) in enumerate(pairs)]
    loads[0].start()
    loads[1].start()

    barrier = pltpu.get_barrier_semaphore()

    for f, l in [(p, lane) for p in peers[1:]] + [(me, l) for l in lanes[1:]]:
        pl.semaphore_signal(barrier, inc=1, device_id=(f, l), device_id_type=MESH)

    loads[0].wait()
    ids = lax.broadcasted_iota(jnp.int32, table.shape, 1)

    def name(j, named):
        return jnp.where(ids == slot[j], j + 1, named)

    table[...] = lax.fori_loop(0, grad.shape[0], name, jnp.zeros(table.shape, jnp.int32))
    move = pltpu.make_async_copy(table, source, in_sem.at[len(pairs)])
    move.start()
    move.wait()
    loads[1].wait()

    for a in range(cap):

        def fill(o, c, a=a):
            named = source[0, o * cap + a]
            chunk = grad[jnp.maximum(named - 1, 0)]
            stage[a, o] = jnp.where(named > 0, chunk, 0.0)
            return c

        lax.fori_loop(0, fs, fill, 0)
        if a == 0:
            pl.semaphore_wait(barrier, fs - 1 + mps - 1)

        def send(d, c, a=a):
            p = peer(d)
            pltpu.make_async_remote_copy(
                src_ref=stage.at[a, p],
                dst_ref=blocks.at[a, rows_of(me)],
                send_sem=fsend.at[a],
                recv_sem=frecv.at[a],
                device_id=(p, lane),
                device_id_type=MESH,
            ).start()
            return c

        lax.fori_loop(1, fs, send, 0)
        blocks[a, rows_of(me)] = stage[a, me]

    for load in loads[2:]:
        load.start()
    for load in loads[2:]:
        load.wait()

    def give_back(a, first, last):
        def send(d, c):
            p = peer(d)
            pltpu.make_async_remote_copy(
                src_ref=dirs.at[a, rows_of(p)],
                dst_ref=back.at[a, me],
                send_sem=rsend.at[a],
                recv_sem=rrecv.at[a],
                device_id=(p, lane),
                device_id_type=MESH,
            ).start()
            return c

        lax.fori_loop(first, last, send, 0)

    def part(t):
        return pl.ds(pl.multiple_of(t * tile, tile), tile)

    def total(x):
        return jnp.sum(x, axis=(0, 1), keepdims=True)

    def precondition(a):
        def cut(t, sq):
            g = blocks[a, part(t)]
            h, l = split(g)
            high[a, part(t)] = h
            low[a, part(t)] = l
            return sq + total(g * g)

        grad_sq = lax.fori_loop(0, tiles, cut, jnp.zeros((1, 1), F32))

        def multiply(t, sq):
            root = lr[a, part(t)]
            h, l = split(dot(root, high[a]) + dot(root, low[a]))
            p = dot(h, rr[a]) + dot(l, rr[a])
            dirs[a, part(t)] = p
            return sq + total(p * p)

        pre_sq = lax.fori_loop(0, tiles, multiply, jnp.zeros((1, 1), F32))
        ratio = jnp.sqrt(grad_sq) / (jnp.sqrt(pre_sq) + epsilon)

        def graft(t, sq):
            p = dirs[a, part(t)] * ratio
            dirs[a, part(t)] = p
            return sq + total(p * p)

        return lax.fori_loop(0, tiles, graft, jnp.zeros((1, 1), F32))

    def statistics(a):
        def left(t, c):
            h, l = high[a, part(t)], low[a, part(t)]
            prod = dot(h, high[a], 1, 1) + dot(h, low[a], 1, 1) + dot(l, high[a], 1, 1)
            ls[a, part(t)] = decay_rate * ls[a, part(t)] + (1.0 - decay_rate) * prod
            return c

        lax.fori_loop(0, tiles, left, 0)
        for t in range(tiles):
            cols = pl.ds(t * tile, tile)
            h, l = high[a, :, cols], low[a, :, cols]
            prod = dot(h, high[a], 0, 0) + dot(h, low[a], 0, 0) + dot(l, high[a], 0, 0)
            rs[a, cols] = decay_rate * rs[a, cols] + (1.0 - decay_rate) * prod

    def wait_for(ref, sem):
        pltpu.make_async_copy(ref, ref, sem).wait()

    others = fs - 1

    def send_square(d, c):
        pltpu.make_async_remote_copy(
            src_ref=sq_out,
            dst_ref=sq_group.at[me],
            send_sem=qsend.at[0],
            recv_sem=qrecv.at[0],
            device_id=(peer(d), lane),
            device_id_type=MESH,
        ).start()
        return c

    def send_sum(d, c):
        pltpu.make_async_remote_copy(
            src_ref=sq_sum,
            dst_ref=sq_all.at[lane],
            send_sem=qsend.at[1],
            recv_sem=qrecv.at[1],
            device_id=(me, (lane + d) % mps),
            device_id_type=MESH,
        ).start()
        return c

    squares = jnp.zeros((1, 1), F32)
    for a in range(cap):
        wait_for(blocks.at[a, pl.ds(0, others * rows)], frecv.at[a])
        squares = squares + precondition(a)
        if a < cap - 1:
            give_back(a, 1, fs)
            statistics(a)
        else:
            sq_out[...] = jnp.broadcast_to(squares, sq_out.shape)
            lax.fori_loop(1, fs, send_square, 0)
            sq_group[me] = sq_out[...]
            give_back(a, 1, fs // 2)
            wait_for(sq_group.at[pl.ds(0, others)], qrecv.at[0])
            sq_sum[...] = jnp.sum(sq_group[...], axis=0)
            lax.fori_loop(1, mps, send_sum, 0)
            sq_all[lane] = sq_sum[...]
            give_back(a, fs // 2, fs)
            statistics(a)
        back[a, me] = dirs[a, rows_of(me)]

    wait_for(sq_all.at[pl.ds(0, mps - 1)], qrecv.at[1])
    total_sq = jnp.sum(sq_all[...], axis=0)
    scale = (1.0 / jnp.sqrt(total_sq / entries + epsilon))[0:1, 0:1]

    for a in range(cap):
        wait_for(stage.at[a, pl.ds(0, others)], fsend.at[a])
        wait_for(dirs.at[a, pl.ds(0, others * rows)], rsend.at[a])
    wait_for(sq_group.at[pl.ds(0, others)], qsend.at[0])
    wait_for(sq_all.at[pl.ds(0, mps - 1)], qsend.at[1])
    for a in range(cap):
        wait_for(back.at[a, pl.ds(0, others)], rrecv.at[a])

    def place(j, c):
        s = slot[j]
        update[j] = back[s % cap, s // cap] * scale
        return c

    lax.fori_loop(0, update.shape[0], place, 0, unroll=4)


def finish(update, ls, rs, update_hbm, nl_hbm, nr_hbm, sem):
    pairs = ((update, update_hbm), (ls, nl_hbm), (rs, nr_hbm))
    stores = [pltpu.make_async_copy(a, b, sem.at[i]) for i, (a, b) in enumerate(pairs)]
    for store in stores:
        store.start()
    for store in stores:
        store.wait()


def far(x):
    return pltpu.with_memory_space_constraint(x, pltpu.HBM)


def local(inner, grad, block_slot, left_stat, right_stat, left_root, right_root):
    fs, mps = lax.axis_size("fsdp"), lax.axis_size("mp")
    cap = left_stat.shape[0]
    count, rows, width = grad.shape
    entries = float(count * mps * width * width)
    square = (cap, width, width)
    chunks = (cap, fs, rows, width)
    table = (1, -(-fs * cap // 128) * 128)
    hbm = pl.BlockSpec(memory_space=pltpu.HBM)
    vmem = pl.BlockSpec(memory_space=pltpu.VMEM)
    update, left, right = pl.pallas_call(
        functools.partial(kernel, (fs, mps, cap, rows, width, inner, entries)),
        out_shape=(
            pltpu.VMEM(grad.shape, F32),
            pltpu.VMEM(square, F32),
            pltpu.VMEM(square, F32),
        ),
        in_specs=[hbm] * 6,
        out_specs=(vmem,) * 3,
        scratch_shapes=[
            pltpu.VMEM(chunks, F32),
            pltpu.SMEM(block_slot.shape, jnp.int32),
            pltpu.VMEM(table, jnp.int32),
            pltpu.SMEM(table, jnp.int32),
            pltpu.VMEM(grad.shape, F32),
            pltpu.VMEM(chunks, F32),
            pltpu.VMEM(square, F32),
            pltpu.VMEM(square, F32),
            pltpu.VMEM(square, BF16),
            pltpu.VMEM(square, BF16),
            pltpu.VMEM(square, BF16),
            pltpu.VMEM(square, BF16),
            pltpu.VMEM((1, 128), F32),
            pltpu.VMEM((fs, 1, 128), F32),
            pltpu.VMEM((1, 128), F32),
            pltpu.VMEM((mps, 1, 128), F32),
            pltpu.SemaphoreType.DMA((7,)),
            pltpu.SemaphoreType.DMA((cap,)),
            pltpu.SemaphoreType.DMA((cap,)),
            pltpu.SemaphoreType.DMA((cap,)),
            pltpu.SemaphoreType.DMA((cap,)),
            pltpu.SemaphoreType.DMA((2,)),
            pltpu.SemaphoreType.DMA((2,)),
        ],
        compiler_params=pltpu.CompilerParams(
            collective_id=0, has_side_effects=True, vmem_limit_bytes=40 << 20
        ),
        cost_estimate=pl.CostEstimate(
            flops=20 * cap * width**3, bytes_accessed=12 << 20, transcendentals=0
        ),
    )(
        far(block_slot),
        far(grad),
        far(left_stat[:, 0]),
        far(right_stat[:, 0]),
        far(left_root[:, 0]),
        far(right_root[:, 0]),
    )
    update, new_left, new_right = pl.pallas_call(
        finish,
        out_shape=(
            jax.ShapeDtypeStruct(grad.shape, F32),
            jax.ShapeDtypeStruct(square, F32),
            jax.ShapeDtypeStruct(square, F32),
        ),
        in_specs=[vmem] * 3,
        out_specs=(hbm,) * 3,
        scratch_shapes=[pltpu.SemaphoreType.DMA((3,))],
        compiler_params=pltpu.CompilerParams(vmem_limit_bytes=16 << 20),
        cost_estimate=pl.CostEstimate(flops=0, bytes_accessed=5 << 20, transcendentals=0),
    )(update, left, right)
    return (update, new_left[:, None], new_right[:, None])


def solution(mesh):
    fs = mesh.shape["fsdp"]
    inner = 8 if fs % 8 == 0 else fs
    placed = (
        P("mp", "fsdp", None),
        P("mp"),
        P("fsdp", "mp", None, None),
        P("fsdp", "mp", None, None),
        P("fsdp", "mp", None, None),
        P("fsdp", "mp", None, None),
    )
    return jax.shard_map(
        functools.partial(local, inner),
        mesh=mesh,
        in_specs=placed,
        out_specs=(P("mp", "fsdp", None), P("fsdp", "mp", None, None), P("fsdp", "mp", None, None)),
        check_vma=False,
    )
```

profile of v0, /device:TPU:32, one launch (start us, length us, event | category | flops | bytes accessed | tf_op | source)
XLA Modules:
  0.0 107.1 jit_solution(5417417837383517822)
XLA Ops:
  0.6 104.1 %shard_map.85 = (f32[32,16,512]{2,1,0:T(8,128)S(1)}, f32[2,512,512]{2,1,0:T(8,128)S(1)}, f32[2,512,512]{2,1,0:T(8,128)S(1)}) custom-call(s32[32]{0:T(128)} %slot_hbm.1, f32[32,16,512]{2,1,0:T(8,128)} %grad_hbm.1, f32[2,512,512]{2,1,0:T(8,128)} %bitcast.10, f32[2,512,512]{2,1,0:T(8,128)} %bitcast.11, bf16[2,512,512]{2,1,0:T(8,128)(2,1)} %bitcast.14, ...), custom_call_target="tpu_custom_call" | custom-call | flops 5368709120 | bytes 12582912 | tf_op jit(solution)/shard_map/pallas_call | solution.py:302
  104.8 2.4 %shard_map.86 = (f32[32,16,512]{2,1,0:T(8,128)}, f32[2,512,512]{2,1,0:T(8,128)}, f32[2,512,512]{2,1,0:T(8,128)}) custom-call(f32[32,16,512]{2,1,0:T(8,128)S(1)} %get-tuple-element.9.update, f32[2,512,512]{2,1,0:T(8,128)S(1)} %get-tuple-element.10.ls, f32[2,512,512]{2,1,0:T(8,128)S(1)} %get-tuple-element.11.rs), custom_call_target="tpu_custom_call" | custom-call | bytes 5242880 | tf_op jit(solution)/shard_map/pallas_call | solution.py:350
where the time goes:
time: 107 us
  Pallas kernels  107 us (100%)
    pallas_call x1, Pallas kernels, local(): pl.pallas_call(functools.partial(kernel, (fs, mps, cap, rows, width, inne...  104 us
    pallas_call x1, Pallas kernels, local(): pl.pallas_call(finish, out_shape=(jax.ShapeDtypeStruct(grad.shape, F32),...  2.38 us

commit v1 on v0

--- a/solution.py
+++ b/solution.py
@@ -244,10 +244,11 @@
             give_back(a, 1, fs)
             statistics(a)
         else:
+            give_back(a, 1, fs // 4)
             sq_out[...] = jnp.broadcast_to(squares, sq_out.shape)
             lax.fori_loop(1, fs, send_square, 0)
             sq_group[me] = sq_out[...]
-            give_back(a, 1, fs // 2)
+            give_back(a, fs // 4, fs // 2)
             wait_for(sq_group.at[pl.ds(0, others)], qrecv.at[0])
             sq_sum[...] = jnp.sum(sq_group[...], axis=0)
             lax.fori_loop(1, mps, send_sum, 0)

time: 107 us -> 107 us (level)
  no operation moved by 1% of the time
where the time goes in v1:
time: 107 us
  Pallas kernels  106 us (99%)
    pallas_call x1, Pallas kernels, local(): pl.pallas_call(functools.partial(kernel, (fs, mps, cap, rows, width, inne...  104 us
    pallas_call x1, Pallas kernels, local(): pl.pallas_call(finish, out_shape=(jax.ShapeDtypeStruct(grad.shape, F32),...  2.38 us

profile of v1, /device:TPU:32, one launch (start us, length us, event | category | flops | bytes accessed | tf_op | source)
XLA Modules:
  0.0 106.9 jit_solution(9627396709438921228)
XLA Ops:
  0.6 103.9 %shard_map.85 = (f32[32,16,512]{2,1,0:T(8,128)S(1)}, f32[2,512,512]{2,1,0:T(8,128)S(1)}, f32[2,512,512]{2,1,0:T(8,128)S(1)}) custom-call(s32[32]{0:T(128)} %slot_hbm.1, f32[32,16,512]{2,1,0:T(8,128)} %grad_hbm.1, f32[2,512,512]{2,1,0:T(8,128)} %bitcast.10, f32[2,512,512]{2,1,0:T(8,128)} %bitcast.11, bf16[2,512,512]{2,1,0:T(8,128)(2,1)} %bitcast.14, ...), custom_call_target="tpu_custom_call" | custom-call | flops 5368709120 | bytes 12582912 | tf_op jit(solution)/shard_map/pallas_call | solution.py:303
  104.6 2.4 %shard_map.86 = (f32[32,16,512]{2,1,0:T(8,128)}, f32[2,512,512]{2,1,0:T(8,128)}, f32[2,512,512]{2,1,0:T(8,128)}) custom-call(f32[32,16,512]{2,1,0:T(8,128)S(1)} %get-tuple-element.9.update, f32[2,512,512]{2,1,0:T(8,128)S(1)} %get-tuple-element.10.ls, f32[2,512,512]{2,1,0:T(8,128)S(1)} %get-tuple-element.11.rs), custom_call_target="tpu_custom_call" | custom-call | bytes 5242880 | tf_op jit(solution)/shard_map/pallas_call | solution.py:351
